TPU v7x, 128 devices: a whole 4x4x4 slice. The times are simulated.
128 devices in a mesh: member: 8 (over z, y_lo), space: 16 (over x, y_hi, core).
Axes of the slice: x: 4, y: 4 (y_hi: 2, y_lo: 2; y = y_hi * 2 + y_lo), z: 4, core: 2. Of those that a mesh axis runs over, the one named last changes fastest.
Arguments:
- ensemble: bfloat16 [256, 524288], P('member', 'space')
- analysis: float32 [524288], P('space'), may hold values from -6 to 6
Outputs:
- scaled_gradient: float32 [256, 524288], P('member', 'space')
All inputs are finite; a program needn't handle non-finite values.
Results may differ from a plain program's by a relative error of at most 0.0003.
Values may be sent and summed in bfloat16 or wider, within the bound.
A program may use at most 128 MiB of HBM per device.

v0:
```python
import math

import jax
import jax.numpy as jnp
from jax import lax
from jax.sharding import PartitionSpec as P


def pair_weights(own_norms, all_norms, cross, row_offset):
    pair_sq = own_norms[:, None] + all_norms[None, :] - 2.0 * cross
    rows_index = lax.broadcasted_iota(jnp.int32, cross.shape, 0) + row_offset
    cols_index = lax.broadcasted_iota(jnp.int32, cross.shape, 1)
    on_diag = rows_index == cols_index
    safe_sq = jnp.where(on_diag, jnp.float32(1.0), pair_sq)
    return jnp.where(on_diag, jnp.float32(0.0), 1.0 / jnp.sqrt(safe_sq))


def finish(values, deviation, obs_sum, row_total, weighted, members, factor):
    obs_dist = jnp.sqrt(obs_sum)
    return factor * (
        deviation / obs_dist[:, None] - (row_total[:, None] * values - weighted) / members
    )


def on_device(ensemble, analysis):
    own_count = ensemble.shape[0]
    point_count = ensemble.shape[1]
    groups = lax.axis_size("member")
    members = own_count * groups
    factor = jnp.float32(math.sqrt(point_count * lax.axis_size("space")))
    values = ensemble.astype(jnp.float32)
    deviation = values - analysis[None, :]
    obs_part = jnp.sum(deviation * deviation, axis=1)
    piece = lax.all_gather(ensemble, "member", axis=0, tiled=True)
    cross_block = jnp.einsum("ap,bp->ab", ensemble, piece, preferred_element_type=jnp.float32)
    piece_norms = jnp.sum(jnp.square(piece.astype(jnp.float32)), axis=1)
    partial_value = jnp.concatenate([cross_block, piece_norms[None, :]], axis=0)
    summed, obs_sum = lax.psum((partial_value, obs_part), "space")
    cross = summed[:own_count]
    all_norms = summed[own_count]
    row_offset = lax.axis_index("member") * own_count
    own_norms = lax.dynamic_slice_in_dim(all_norms, row_offset, own_count)
    weights = pair_weights(own_norms, all_norms, cross, row_offset)
    row_total = jnp.sum(weights, axis=1)
    low_weights = weights.astype(jnp.bfloat16)
    weighted = jnp.dot(
        low_weights,
        lax.all_gather(ensemble, "member", axis=0, tiled=True),
        preferred_element_type=jnp.float32,
    )
    return finish(values, deviation, obs_sum, row_total, weighted, members, factor)


def solution(mesh):
    placed = (P("member", "space"), P("space"))
    return jax.shard_map(
        on_device, mesh=mesh, in_specs=placed, out_specs=P("member", "space"), check_vma=False
    )
```

profile of v0, /device:TPU:0, one launch (start us, length us, event | category | flops | bytes accessed | tf_op | source)
XLA Modules:
  0.0 442.8 jit_solution(1457313893297209832)
XLA Ops:
  6.5 0.0 all-gather.2.cloned.1.call-start
  6.5 0.7 all-gather.2.cloned.1.call-update
  7.3 2.2 fusion.5
  9.5 0.0 copy-start
  9.5 327.6 %all-gather.2.cloned.1.call-done = bf16[256,32768]{1,0:T(8,128)(2,1)} async-done(((bf16[32,32768]{1,0:T(8,128)(2,1)}), bf16[256,32768]{1,0:T(8,128)(2,1)}) %all-gather.2.cloned.1.call-update) | async-done | bytes 16777232 | tf_op jit(solution)/shard_map/all_gather | solution.py:34
  337.1 7.2 %multiply_reduce_fusion = f32[256]{0:T(256)S(1)} fusion(bf16[256,32768]{1,0:T(8,128)(2,1)} %all-gather.2.cloned.1.call-done), kind=kLoop, calls=%fused_computation.4 | loop fusion | flops 25165568 | bytes 16778240 | tf_op jit(solution)/shard_map/reduce_sum | solution.py:36
  344.3 0.0 copy-done
  344.3 0.0 copy-start.1
  344.3 10.9 %fusion.22 = f32[32,256]{1,0:T(8,128)S(1)} fusion(bf16[32,32768]{1,0:T(8,128)(2,1)S(1)} %copy-done, bf16[256,32768]{1,0:T(8,128)(2,1)} %all-gather.2.cloned.1.call-done), kind=kOutput, calls=%fused_computation.30 | convolution fusion | flops 536870912 | bytes 18907136 | tf_op jit(solution)/shard_map/ap,bp->ab/dot_general | solution.py:35
  355.3 69.2 %all-reduce = (f32[33,256]{1,0:T(8,128)S(1)}, f32[32]{0:T(128)S(1)}) all-reduce(f32[33,256]{1,0:T(8,128)S(1)} %pad_maximum_fusion, f32[32]{0:T(128)S(1)} %fusion.5), channel_id=1, replica_groups=mesh['member'=8,'space'=16] {'space'}, use_global_device_ids=true, to_apply=%region_3.0 | all-reduce | flops 8480 | bytes 67840 | tf_op jit(solution)/shard_map/psum | solution.py:38
  424.5 0.1 dynamic-slice_bitcast_fusion
  424.5 0.2 fusion.11
  424.7 0.0 copy-done.1
  424.7 11.2 %fusion.2 = f32[32,32768]{1,0:T(8,128)} fusion(bf16[256,32768]{1,0:T(8,128)(2,1)} %all-gather.2.cloned.1.call-done, bf16[32,32768]{1,0:T(8,128)(2,1)S(1)} %copy-done, f32[32]{0:T(128)S(1)} %fusion.11, f32[32]{0:T(128)S(1)} %sqrt.6, f32[32768]{0:T(1024)S(1)} %copy-done.1, f32[33,256]{1,0:T(8,128)S(1)} %get-tuple-element.5, f32[256]{0:T(256)S(1)} %bitcast.9, ...), kind=kOutput, calls=%fused_computation.3 | convolution fusion | flops 545316864 | bytes 23235584 | tf_op jit(solution)/shard_map/dot_general | solution.py:46
  (4 shorter events, 0.0 us)
Async XLA Ops:
  6.5 330.6 %all-gather.2.cloned.1.call-start = ((), (), s32[]{:S(2)}) async-start(), calls=%async_computation | async-start | bytes 18874368 | tf_op jit(solution)/shard_map/all_gather | solution.py:34
  9.5 334.8 %copy-start = (bf16[32,32768]{1,0:T(8,128)(2,1)S(1)}, bf16[32,32768]{1,0:T(8,128)(2,1)}, u32[]{:S(2)}) copy-start(bf16[32,32768]{1,0:T(8,128)(2,1)} %param.2) | copy-start | bytes 6291460
  344.3 80.4 %copy-start.1 = (f32[32768]{0:T(1024)S(1)}, f32[32768]{0:T(1024)}, u32[]{:S(2)}) copy-start(f32[32768]{0:T(1024)} %param.3) | copy-start | bytes 393220
Sparse Core Ops, SparseCore 0:
  9.0 328.0 all-gather.1
where the time goes:
time: 443 us
  waiting for transfers between devices  328 us (74%)
  blocking collectives  69.2 us (16%)
  matrix products  22.1 us (5%)
  between operations  13.5 us (3%)
  other arithmetic  9.63 us (2%)
    all_gather x1, waiting for transfers between devices, on_device(): piece = lax.all_gather(ensemble, 'member', axis=0, tiled=True)  328 us
    psum x1, blocking collectives, on_device(): summed, obs_sum = lax.psum((partial_value, obs_part), 'space')  69.2 us
    dot_general x1, matrix products, on_device(): jnp.dot(low_weights, lax.all_gather(ensemble, 'member', axis=0, tiled=Tru...  11.2 us
    dot_general x1, matrix products, on_device(): jnp.einsum('ap,bp->ab', ensemble, piece, preferred_element_type=jnp.float32)  10.9 us
  transfers between devices with their start and end apart: 1, of which 1 were waited for; matrix products, arithmetic and copies ran while one was open for 1% of the time, Pallas kernels for 0%

commit v1 on v0

v1 whole, which is shorter than its diff:
```python
import functools
import math

import jax
import jax.numpy as jnp
from jax import lax
from jax.experimental import pallas as pl
from jax.experimental.pallas import tpu as pltpu
from jax.sharding import PartitionSpec as P

MESH = pl.DeviceIdType.MESH
F32 = jnp.float32
BF16 = jnp.bfloat16
RANGE = 250.0
SHIFT = 125.0
LN2 = math.log(2.0)
CHUNK = 512


def chunk_at(index):
    return pl.ds(pl.multiple_of(index * CHUNK, CHUNK), CHUNK)


def kernel(
    groups, chips, factor, x_hbm, a_hbm, out_hbm,
    gathered, own, analysis, weighted, sent, got, staged,
    part, part_in, chip_in, summed, low, totals, norms, obs_in,
    x_send, x_recv, p_send, p_recv, c_send, c_recv, s_send, s_recv, r_send, r_recv,
    o_send, o_recv, out_sem, local_sem,
):
    me = lax.axis_index("member")
    place = lax.axis_index("space")
    core = lax.rem(place, 2)
    chip = place // 2
    rank = me * 2 + core
    teams = groups * 2
    rows = own.shape[0]
    cols = gathered.shape[2]
    members = groups * rows
    steps = cols // CHUNK

    def columns(index):
        return pl.ds(pl.multiple_of(index * cols, cols), cols)

    def group_peer(d):
        other = lax.rem(me + d, groups)
        return other, (other, place)

    def team_peer(d):
        other = lax.rem(rank + d, teams)
        return other, (other // 2, chip * 2 + lax.rem(other, 2))

    def chip_peer(d):
        other = lax.rem(chip + d, chips)
        return other, (me, other * 2 + core)

    sibling = (me, chip * 2 + 1 - core)

    def remote(src, dst, send, recv, device):
        return pltpu.make_async_remote_copy(
            src_ref=src, dst_ref=dst, send_sem=send, recv_sem=recv,
            device_id=device, device_id_type=MESH,
        )

    load_analysis = pltpu.make_async_copy(a_hbm, analysis, local_sem.at[0])
    load_analysis.start()
    load_own = pltpu.make_async_copy(x_hbm, own, local_sem.at[1])
    load_own.start()
    keep = pltpu.make_async_copy(x_hbm.at[:, columns(me)], gathered.at[me], local_sem.at[2])
    keep.start()

    barrier = pltpu.get_barrier_semaphore()
    for d in range(1, teams):
        pl.semaphore_signal(barrier, inc=1, device_id=team_peer(d)[1], device_id_type=MESH)
    for d in range(1, chips):
        pl.semaphore_signal(barrier, inc=1, device_id=chip_peer(d)[1], device_id_type=MESH)
    pl.semaphore_wait(barrier, teams - 1 + chips - 1)

    spread = []
    for d in range(1, groups):
        other, device = group_peer(d)
        copy = remote(
            x_hbm.at[:, columns(other)], gathered.at[me], x_send.at[d], x_recv.at[d], device
        )
        copy.start()
        spread.append(copy)

    load_analysis.wait()
    load_own.wait()

    def add_distance(i, total):
        at = chunk_at(i)
        deviation = own[:, at].astype(F32) - analysis[:, at]
        square = deviation * deviation
        for k in range(CHUNK // 128):
            total = total + square[:, k * 128:(k + 1) * 128]
        return total

    distance = lax.fori_loop(0, own.shape[1] // CHUNK, add_distance, jnp.zeros((rows, 128), F32))
    obs_in[chips] = distance
    pair = remote(obs_in.at[chips], obs_in.at[chips + 1], o_send.at[0], o_recv.at[0], sibling)
    pair.start()
    pair.wait()
    obs_in[chip] = distance + obs_in[chips + 1]
    obs_copies = []
    for d in range(1, chips):
        other, device = chip_peer(d)
        copy = remote(obs_in.at[chip], obs_in.at[chip], o_send.at[d], o_recv.at[d], device)
        copy.start()
        obs_copies.append(copy)

    keep.wait()
    for copy in spread:
        copy.wait()

    def add_products(i, total):
        block = gathered[:, :, chunk_at(i)].reshape(members, CHUNK)
        return total + lax.dot_general(
            block, block, (((1,), (1,)), ((), ())), preferred_element_type=F32
        )

    cross = lax.fori_loop(0, steps, add_products, jnp.zeros((members, members), F32))
    row_index = lax.broadcasted_iota(jnp.int32, (members, members), 0)
    col_index = lax.broadcasted_iota(jnp.int32, (members, members), 1)
    diagonal = jnp.where(row_index == col_index, cross, 0.0)
    norm_rows = jnp.sum(diagonal, axis=1, keepdims=True)
    norm_cols = jnp.sum(diagonal, axis=0, keepdims=True)
    norms[...] = jnp.broadcast_to(norm_rows, (members, 128)).reshape(groups, rows, 128)
    pair_sq = norm_rows + norm_cols - 2.0 * cross
    half = members // 2
    small_row = lax.broadcasted_iota(jnp.int32, (half, half), 0)
    small_col = lax.broadcasted_iota(jnp.int32, (half, half), 1)
    upper = small_col > small_row
    lower = small_col < small_row
    share = members // teams
    part[: teams // 2] = pair_sq[:half, half:].reshape(teams // 2, share, half)
    part[teams // 2 :] = jnp.where(upper, pair_sq[:half, :half], pair_sq[half:, half:]).reshape(
        teams // 2, share, half
    )

    copies = []
    for d in range(1, teams):
        other, device = team_peer(d)
        copy = remote(part.at[other], part_in.at[rank], p_send.at[d], p_recv.at[d], device)
        copy.start()
        copies.append(copy)
    part_in[rank] = part[rank]
    for copy in copies:
        copy.wait()
    chip_in[chip] = jnp.sum(part_in[...], axis=0)
    copies = []
    for d in range(1, chips):
        other, device = chip_peer(d)
        copy = remote(chip_in.at[chip], chip_in.at[chip], c_send.at[d], c_recv.at[d], device)
        copy.start()
        copies.append(copy)
    for copy in copies:
        copy.wait()
    summed[rank] = jnp.sum(chip_in[...], axis=0)
    copies = []
    for d in range(1, teams):
        other, device = team_peer(d)
        copy = remote(summed.at[rank], summed.at[rank], s_send.at[d], s_recv.at[d], device)
        copy.start()
        copies.append(copy)
    for copy in copies:
        copy.wait()

    off = 1.0 / jnp.sqrt(summed[: teams // 2].reshape(half, half))
    triangles = summed[teams // 2 :].reshape(half, half)
    triangles = jnp.where(small_row == small_col, 1.0, triangles)
    triangles = 1.0 / jnp.sqrt(triangles)
    above = jnp.where(upper, triangles, 0.0)
    below = jnp.where(lower, triangles, 0.0)
    first = above + above.T
    second = below + below.T
    off_t = off.T
    low[:half, :half] = first.astype(BF16)
    low[:half, half:] = off.astype(BF16)
    low[half:, :half] = off_t.astype(BF16)
    low[half:, half:] = second.astype(BF16)
    total_first = jnp.sum(first + off, axis=1, keepdims=True)
    total_second = jnp.sum(second + off_t, axis=1, keepdims=True)
    groups_half = groups // 2
    totals[:groups_half] = jnp.broadcast_to(total_first, (half, 128)).reshape(groups_half, rows, 128)
    totals[groups_half:] = jnp.broadcast_to(total_second, (half, 128)).reshape(
        groups_half, rows, 128
    )

    def weigh(i, total):
        at = chunk_at(i)
        block = gathered[:, :, at].reshape(members, CHUNK)
        product = jnp.dot(low[...], block, preferred_element_type=F32)
        weighted[:, :, at] = product.reshape(groups, rows, CHUNK)
        along = product * block.astype(F32)
        for k in range(CHUNK // 128):
            total = total + along[:, k * 128:(k + 1) * 128]
        return total

    along = lax.fori_loop(0, steps, weigh, jnp.zeros((members, 128), F32))
    along = jnp.sum(along, axis=1, keepdims=True)
    square = norms[...].reshape(members, 128)[:, :1]
    slopes = jnp.where(square > 0.0, along / jnp.where(square > 0.0, square, 1.0), 0.0)
    slopes = slopes.astype(BF16).astype(F32)
    norms[...] = jnp.broadcast_to(slopes, (members, 128)).reshape(groups, rows, 128)

    returns = []
    for d in range(1, groups):
        other, device = group_peer(d)
        slope = norms[other][:, :1]

        def largest(i, top, other=other, slope=slope):
            at = chunk_at(i)
            rest = weighted[other, :, at] - slope * gathered[other, :, at].astype(F32)
            weighted[other, :, at] = rest
            rest = jnp.abs(rest)
            for k in range(CHUNK // 128):
                top = jnp.maximum(top, rest[:, k * 128:(k + 1) * 128])
            return top

        top = lax.fori_loop(0, steps, largest, jnp.zeros((rows, 128), F32))
        top = jnp.max(top, axis=1, keepdims=True)
        scale = jnp.maximum(top * 1.0079, 1e-30).astype(BF16).astype(F32)
        inverse = RANGE / scale

        def code(i, _, other=other, inverse=inverse):
            at = chunk_at(i)
            rest = weighted[other, :, at]
            size = jnp.exp2(jnp.abs(rest) * inverse - SHIFT)
            sent[other, :, at] = jnp.where(rest < 0.0, -size, size).astype(BF16)
            return 0

        lax.fori_loop(0, steps, code, 0)
        lane = lax.broadcasted_iota(jnp.int32, (rows, 128), 1)
        sent[other, :, cols:] = jnp.where(lane < 64, scale, slope).astype(BF16)
        copy = remote(sent.at[other], got.at[me], r_send.at[d], r_recv.at[d], device)
        copy.start()
        returns.append(copy)

    for copy in obs_copies:
        copy.wait()
    obs = jnp.sqrt(jnp.sum(jnp.sum(obs_in[:chips], axis=0), axis=1, keepdims=True))
    near = factor / obs
    row_total = totals[me][:, :1]

    def finish(piece, along_own, value_at):
        def one(i, _):
            at = chunk_at(i)
            point = pl.ds(pl.multiple_of(piece * cols + i * CHUNK, CHUNK), CHUNK)
            values = own[:, point].astype(F32)
            spread_term = value_at(at) - along_own * values
            staged[:, point] = (values - analysis[:, point]) * near + spread_term * (factor / members)
            return 0

        lax.fori_loop(0, steps, one, 0)
        copy = pltpu.make_async_copy(
            staged.at[:, columns(piece)], out_hbm.at[:, columns(piece)], out_sem.at[piece]
        )
        copy.start()

    finish(me, row_total, lambda at: weighted[me, :, at])
    for d in range(1, groups):
        returns[d - 1].wait()
        piece = lax.rem(me + groups - d, groups)
        scale = got[piece, :, cols:cols + 1].astype(F32) * (1.0 / (RANGE * LN2))
        slope = got[piece, :, cols + 64:cols + 65].astype(F32)

        def decode(at, piece=piece, scale=scale):
            coded = got[piece, :, at].astype(F32)
            size = (jnp.log(jnp.abs(coded)) + SHIFT * LN2) * scale
            return jnp.where(coded < 0.0, -size, size)

        finish(piece, row_total - slope, decode)
    for piece in range(groups):
        at = pl.ds(piece * cols, cols)
        pltpu.make_async_copy(staged.at[:, at], out_hbm.at[:, at], out_sem.at[piece]).wait()


def on_device(ensemble, analysis):
    rows, points = ensemble.shape
    groups = lax.axis_size("member")
    places = lax.axis_size("space")
    chips = places // 2
    teams = groups * 2
    members = rows * groups
    cols = points // groups
    half = members // 2
    share = members // teams
    factor = math.sqrt(points * places)
    dma = pltpu.SemaphoreType.DMA
    return pl.pallas_call(
        functools.partial(kernel, groups, chips, factor),
        out_shape=jax.ShapeDtypeStruct((rows, points), F32),
        in_specs=[pl.BlockSpec(memory_space=pltpu.HBM)] * 2,
        out_specs=pl.BlockSpec(memory_space=pltpu.HBM),
        scratch_shapes=[
            pltpu.VMEM((groups, rows, cols), BF16),
            pltpu.VMEM((rows, points), BF16),
            pltpu.VMEM((1, points), F32),
            pltpu.VMEM((groups, rows, cols), F32),
            pltpu.VMEM((groups, rows, cols + 128), BF16),
            pltpu.VMEM((groups, rows, cols + 128), BF16),
            pltpu.VMEM((rows, points), F32),
            pltpu.VMEM((teams, share, half), F32),
            pltpu.VMEM((teams, share, half), F32),
            pltpu.VMEM((chips, share, half), F32),
            pltpu.VMEM((teams, share, half), F32),
            pltpu.VMEM((members, members), BF16),
            pltpu.VMEM((groups, rows, 128), F32),
            pltpu.VMEM((groups, rows, 128), F32),
            pltpu.VMEM((chips + 2, rows, 128), F32),
            dma((groups,)), dma((groups,)),
            dma((teams,)), dma((teams,)),
            dma((chips,)), dma((chips,)),
            dma((teams,)), dma((teams,)),
            dma((groups,)), dma((groups,)),
            dma((chips,)), dma((chips,)),
            dma((groups,)), dma((3,)),
        ],
        compiler_params=pltpu.CompilerParams(
            collective_id=0, has_side_effects=True, vmem_limit_bytes=48 * 2**20
        ),
        cost_estimate=pl.CostEstimate(
            flops=4 * members * members * cols, bytes_accessed=8 * rows * points, transcendentals=0
        ),
    )(ensemble, analysis.reshape(1, points))


def solution(mesh):
    placed = (P("member", "space"), P("space"))
    return jax.shard_map(
        on_device, mesh=mesh, in_specs=placed, out_specs=P("member", "space"), check_vma=False
    )
```

time: 443 us -> 94.2 us (0.21)
  waiting for transfers between devices: 328 us -> 0 us
  Pallas kernels: 0 us -> 85.3 us
  blocking collectives: 69.2 us -> 0 us
  matrix products: 22.1 us -> 0 us
  between operations: 13.5 us -> 0.01 us
  other arithmetic: 9.63 us -> 0 us
  local copies, waits for them, and re-layouts: 0.1 us -> 6.97 us
    all_gather x1 -> x0, waiting for transfers between devices: 328 us -> none  [on_device(): piece = lax.all_gather(ensemble, 'member', axis=0, tiled=True)]
    pallas_call x0 -> x1, Pallas kernels: none -> 85.3 us  [on_device(): pl.pallas_call(functools.partial(kernel, groups, chips, factor), out_shap...]
    psum x1 -> x0, blocking collectives: 69.2 us -> none  [on_device(): summed, obs_sum = lax.psum((partial_value, obs_part), 'space')]
    dot_general x2 -> x0, matrix products: 22.1 us -> none  [the longest x1 11.2 us: on_device(): jnp.dot(low_weights, lax.all_gather(ensemble, 'member', axis=0, tiled=Tru...]
    reduce_sum x3 -> x0, other arithmetic: 9.62 us -> none  [the longest x1 7.19 us: on_device(): piece_norms = jnp.sum(jnp.square(piece.astype(jnp.float32)), axis=1)]
    unnamed x4 -> x5, local copies, waits for them, and re-layouts: 0.01 us -> 6.97 us
  transfers between devices with their start and end apart: 1 -> 0, of which waited for: 1 -> 0; matrix products, arithmetic and copies ran while one was open for 1% -> 0% of each run, Pallas kernels for 0% -> 0%
where the time goes in v1:
time: 94.2 us; the launch traced here: 92.3 us
  Pallas kernels  85.3 us (91%)
  local copies, waits for them, and re-layouts  6.97 us (7%)
    pallas_call x1, Pallas kernels, on_device(): pl.pallas_call(functools.partial(kernel, groups, chips, factor), out_shap...  85.3 us
    unnamed x5, local copies, waits for them, and re-layouts  6.97 us

profile of v1, /device:TPU:0, one launch (start us, length us, event | category | flops | bytes accessed | tf_op | source)
XLA Modules:
  0.0 92.3 jit_solution(16913302440528792124)
XLA Ops:
  0.0 0.0 copy-start
  0.0 1.6 %copy-done = bf16[32,32768]{1,0:T(8,128)(2,1)S(1)} copy-done((bf16[32,32768]{1,0:T(8,128)(2,1)S(1)}, bf16[32,32768]{1,0:T(8,128)(2,1)}, u32[]{:S(2)}) %copy-start) | copy-done | bytes 2097176
  1.6 0.0 copy-start.1
  1.6 0.9 copy-done.1
  2.5 85.3 %shard_map.28 = f32[32,32768]{1,0:T(8,128)} custom-call(bf16[32,32768]{1,0:T(8,128)(2,1)S(1)} %copy-done, f32[1,32768]{1,0:T(1,128)S(1)} %bitcast.1), custom_call_target="tpu_custom_call" | custom-call | flops 1073741824 | bytes 8388608 | tf_op jit(solution)/shard_map/pallas_call | solution.py:291
  87.8 4.5 %copy.4 = f32[32,32768]{1,0:T(8,128)} copy(f32[32,32768]{1,0:T(8,128)} %shard_map.28) | data formatting | bytes 8388608
Async XLA Ops:
  0.0 1.6 %copy-start = (bf16[32,32768]{1,0:T(8,128)(2,1)S(1)}, bf16[32,32768]{1,0:T(8,128)(2,1)}, u32[]{:S(2)}) copy-start(bf16[32,32768]{1,0:T(8,128)(2,1)} %x_hbm.1) | copy-start | bytes 6291460
  1.6 0.9 copy-start.1

commit v2 on v1

--- a/solution.py
+++ b/solution.py
@@ -15,6 +15,7 @@
 SHIFT = 125.0
 LN2 = math.log(2.0)
 CHUNK = 512
+PARTS = 2
 
 
 def chunk_at(index):
@@ -22,11 +23,11 @@
 
 
 def kernel(
-    groups, chips, factor, x_hbm, a_hbm, out_hbm,
-    gathered, own, analysis, weighted, sent, got, staged,
-    part, part_in, chip_in, summed, low, totals, norms, obs_in,
+    groups, chips, factor, x_hbm, a_hbm, out,
+    gathered, own, analysis, weighted, sent, got,
+    products, part, part_in, chip_in, summed, low, totals, lines, obs_in,
     x_send, x_recv, p_send, p_recv, c_send, c_recv, s_send, s_recv, r_send, r_recv,
-    o_send, o_recv, out_sem, local_sem,
+    o_send, o_recv, local_sem,
 ):
     me = lax.axis_index("member")
     place = lax.axis_index("space")
@@ -37,7 +38,8 @@
     rows = own.shape[0]
     cols = gathered.shape[2]
     members = groups * rows
-    steps = cols // CHUNK
+    width = cols // PARTS
+    steps = width // CHUNK
 
     def columns(index):
         return pl.ds(pl.multiple_of(index * cols, cols), cols)
@@ -77,13 +79,16 @@
     pl.semaphore_wait(barrier, teams - 1 + chips - 1)
 
     spread = []
-    for d in range(1, groups):
-        other, device = group_peer(d)
-        copy = remote(
-            x_hbm.at[:, columns(other)], gathered.at[me], x_send.at[d], x_recv.at[d], device
-        )
-        copy.start()
-        spread.append(copy)
+    for part_at in range(PARTS):
+        for d in range(1, groups):
+            other, device = group_peer(d)
+            src = pl.ds(pl.multiple_of(other * cols + part_at * width, width), width)
+            copy = remote(
+                x_hbm.at[:, src], gathered.at[me, :, pl.ds(part_at * width, width)],
+                x_send.at[part_at * groups + d], x_recv.at[part_at * groups + d], device,
+            )
+            copy.start()
+            spread.append(copy)
 
     load_analysis.wait()
     load_own.wait()
@@ -110,22 +115,27 @@
         obs_copies.append(copy)
 
     keep.wait()
-    for copy in spread:
-        copy.wait()
-
-    def add_products(i, total):
+
+    def add_products(i, _):
         block = gathered[:, :, chunk_at(i)].reshape(members, CHUNK)
-        return total + lax.dot_general(
+        products[...] += lax.dot_general(
             block, block, (((1,), (1,)), ((), ())), preferred_element_type=F32
         )
-
-    cross = lax.fori_loop(0, steps, add_products, jnp.zeros((members, members), F32))
+        return 0
+
+    products[...] = jnp.zeros_like(products)
+    for part_at in range(PARTS):
+        for copy in spread[part_at * (groups - 1):(part_at + 1) * (groups - 1)]:
+            copy.wait_recv()
+        lax.fori_loop(part_at * steps, (part_at + 1) * steps, add_products, 0)
+    for copy in spread:
+        copy.wait_send()
+    cross = products[...]
     row_index = lax.broadcasted_iota(jnp.int32, (members, members), 0)
     col_index = lax.broadcasted_iota(jnp.int32, (members, members), 1)
     diagonal = jnp.where(row_index == col_index, cross, 0.0)
     norm_rows = jnp.sum(diagonal, axis=1, keepdims=True)
     norm_cols = jnp.sum(diagonal, axis=0, keepdims=True)
-    norms[...] = jnp.broadcast_to(norm_rows, (members, 128)).reshape(groups, rows, 128)
     pair_sq = norm_rows + norm_cols - 2.0 * cross
     half = members // 2
     small_row = lax.broadcasted_iota(jnp.int32, (half, half), 0)
@@ -187,55 +197,63 @@
         groups_half, rows, 128
     )
 
-    def weigh(i, total):
+    def weigh(i, carry):
+        along, square = carry
         at = chunk_at(i)
         block = gathered[:, :, at].reshape(members, CHUNK)
         product = jnp.dot(low[...], block, preferred_element_type=F32)
         weighted[:, :, at] = product.reshape(groups, rows, CHUNK)
-        along = product * block.astype(F32)
+        values = block.astype(F32)
+        product = product * values
+        values = values * values
         for k in range(CHUNK // 128):
-            total = total + along[:, k * 128:(k + 1) * 128]
-        return total
-
-    along = lax.fori_loop(0, steps, weigh, jnp.zeros((members, 128), F32))
-    along = jnp.sum(along, axis=1, keepdims=True)
-    square = norms[...].reshape(members, 128)[:, :1]
-    slopes = jnp.where(square > 0.0, along / jnp.where(square > 0.0, square, 1.0), 0.0)
-    slopes = slopes.astype(BF16).astype(F32)
-    norms[...] = jnp.broadcast_to(slopes, (members, 128)).reshape(groups, rows, 128)
+            along = along + product[:, k * 128:(k + 1) * 128]
+            square = square + values[:, k * 128:(k + 1) * 128]
+        return along, square
 
     returns = []
-    for d in range(1, groups):
-        other, device = group_peer(d)
-        slope = norms[other][:, :1]
-
-        def largest(i, top, other=other, slope=slope):
-            at = chunk_at(i)
-            rest = weighted[other, :, at] - slope * gathered[other, :, at].astype(F32)
-            weighted[other, :, at] = rest
-            rest = jnp.abs(rest)
-            for k in range(CHUNK // 128):
-                top = jnp.maximum(top, rest[:, k * 128:(k + 1) * 128])
-            return top
-
-        top = lax.fori_loop(0, steps, largest, jnp.zeros((rows, 128), F32))
-        top = jnp.max(top, axis=1, keepdims=True)
-        scale = jnp.maximum(top * 1.0079, 1e-30).astype(BF16).astype(F32)
-        inverse = RANGE / scale
-
-        def code(i, _, other=other, inverse=inverse):
-            at = chunk_at(i)
-            rest = weighted[other, :, at]
-            size = jnp.exp2(jnp.abs(rest) * inverse - SHIFT)
-            sent[other, :, at] = jnp.where(rest < 0.0, -size, size).astype(BF16)
-            return 0
-
-        lax.fori_loop(0, steps, code, 0)
-        lane = lax.broadcasted_iota(jnp.int32, (rows, 128), 1)
-        sent[other, :, cols:] = jnp.where(lane < 64, scale, slope).astype(BF16)
-        copy = remote(sent.at[other], got.at[me], r_send.at[d], r_recv.at[d], device)
-        copy.start()
-        returns.append(copy)
+    for part_at in range(PARTS):
+        first_step, last_step = part_at * steps, (part_at + 1) * steps
+        zeros = jnp.zeros((members, 128), F32)
+        along, square = lax.fori_loop(first_step, last_step, weigh, (zeros, zeros))
+        along = jnp.sum(along, axis=1, keepdims=True)
+        square = jnp.sum(square, axis=1, keepdims=True)
+        slopes = jnp.where(square > 0.0, along / jnp.where(square > 0.0, square, 1.0), 0.0)
+        slopes = slopes.astype(BF16).astype(F32)
+        lines[...] = jnp.broadcast_to(slopes, (members, 128)).reshape(groups, rows, 128)
+        for d in range(1, groups):
+            other, device = group_peer(d)
+            slope = lines[other][:, :1]
+
+            def largest(i, top, other=other, slope=slope):
+                at = chunk_at(i)
+                rest = weighted[other, :, at] - slope * gathered[other, :, at].astype(F32)
+                weighted[other, :, at] = rest
+                rest = jnp.abs(rest)
+                for k in range(CHUNK // 128):
+                    top = jnp.maximum(top, rest[:, k * 128:(k + 1) * 128])
+                return top
+
+            top = lax.fori_loop(first_step, last_step, largest, jnp.zeros((rows, 128), F32))
+            top = jnp.max(top, axis=1, keepdims=True)
+            scale = jnp.maximum(top * 1.0079, 1e-30).astype(BF16).astype(F32)
+            inverse = RANGE / scale
+
+            def code(i, _, other=other, inverse=inverse, part_at=part_at):
+                rest = weighted[other, :, chunk_at(i + part_at * steps)]
+                size = jnp.exp2(jnp.abs(rest) * inverse - SHIFT)
+                sent[part_at, other, :, chunk_at(i)] = jnp.where(rest < 0.0, -size, size).astype(BF16)
+                return 0
+
+            lax.fori_loop(0, steps, code, 0)
+            lane = lax.broadcasted_iota(jnp.int32, (rows, 128), 1)
+            sent[part_at, other, :, width:] = jnp.where(lane < 64, scale, slope).astype(BF16)
+            at = part_at * groups + d
+            copy = remote(
+                sent.at[part_at, other], got.at[part_at, me], r_send.at[at], r_recv.at[at], device
+            )
+            copy.start()
+            returns.append(copy)
 
     for copy in obs_copies:
         copy.wait()
@@ -243,37 +261,30 @@
     near = factor / obs
     row_total = totals[me][:, :1]
 
-    def finish(piece, along_own, value_at):
+    def finish(piece, offset, count, along_own, value_at):
         def one(i, _):
-            at = chunk_at(i)
-            point = pl.ds(pl.multiple_of(piece * cols + i * CHUNK, CHUNK), CHUNK)
+            point = pl.ds(pl.multiple_of(piece * cols + offset + i * CHUNK, CHUNK), CHUNK)
             values = own[:, point].astype(F32)
-            spread_term = value_at(at) - along_own * values
-            staged[:, point] = (values - analysis[:, point]) * near + spread_term * (factor / members)
+            spread_term = value_at(chunk_at(i)) - along_own * values
+            out[:, point] = (values - analysis[:, point]) * near + spread_term * (factor / members)
             return 0
 
-        lax.fori_loop(0, steps, one, 0)
-        copy = pltpu.make_async_copy(
-            staged.at[:, columns(piece)], out_hbm.at[:, columns(piece)], out_sem.at[piece]
-        )
-        copy.start()
-
-    finish(me, row_total, lambda at: weighted[me, :, at])
-    for d in range(1, groups):
-        returns[d - 1].wait()
-        piece = lax.rem(me + groups - d, groups)
-        scale = got[piece, :, cols:cols + 1].astype(F32) * (1.0 / (RANGE * LN2))
-        slope = got[piece, :, cols + 64:cols + 65].astype(F32)
-
-        def decode(at, piece=piece, scale=scale):
-            coded = got[piece, :, at].astype(F32)
-            size = (jnp.log(jnp.abs(coded)) + SHIFT * LN2) * scale
-            return jnp.where(coded < 0.0, -size, size)
-
-        finish(piece, row_total - slope, decode)
-    for piece in range(groups):
-        at = pl.ds(piece * cols, cols)
-        pltpu.make_async_copy(staged.at[:, at], out_hbm.at[:, at], out_sem.at[piece]).wait()
+        lax.fori_loop(0, count, one, 0)
+
+    finish(me, 0, cols // CHUNK, row_total, lambda at: weighted[me, :, at])
+    for part_at in range(PARTS):
+        for d in range(1, groups):
+            returns[part_at * (groups - 1) + d - 1].wait()
+            piece = lax.rem(me + groups - d, groups)
+            scale = got[part_at, piece, :, width:width + 1].astype(F32) * (1.0 / (RANGE * LN2))
+            slope = got[part_at, piece, :, width + 64:width + 65].astype(F32)
+
+            def decode(at, piece=piece, scale=scale, part_at=part_at):
+                coded = got[part_at, piece, :, at].astype(F32)
+                size = (jnp.log(jnp.abs(coded)) + SHIFT * LN2) * scale
+                return jnp.where(coded < 0.0, -size, size)
+
+            finish(piece, part_at * width, steps, row_total - slope, decode)
 
 
 def on_device(ensemble, analysis):
@@ -290,17 +301,17 @@
     dma = pltpu.SemaphoreType.DMA
     return pl.pallas_call(
         functools.partial(kernel, groups, chips, factor),
-        out_shape=jax.ShapeDtypeStruct((rows, points), F32),
+        out_shape=pltpu.VMEM((rows, points), F32),
         in_specs=[pl.BlockSpec(memory_space=pltpu.HBM)] * 2,
-        out_specs=pl.BlockSpec(memory_space=pltpu.HBM),
+        out_specs=pl.BlockSpec(memory_space=pltpu.VMEM),
         scratch_shapes=[
             pltpu.VMEM((groups, rows, cols), BF16),
             pltpu.VMEM((rows, points), BF16),
             pltpu.VMEM((1, points), F32),
             pltpu.VMEM((groups, rows, cols), F32),
-            pltpu.VMEM((groups, rows, cols + 128), BF16),
-            pltpu.VMEM((groups, rows, cols + 128), BF16),
-            pltpu.VMEM((rows, points), F32),
+            pltpu.VMEM((PARTS, groups, rows, cols // PARTS + 128), BF16),
+            pltpu.VMEM((PARTS, groups, rows, cols // PARTS + 128), BF16),
+            pltpu.VMEM((members, members), F32),
             pltpu.VMEM((teams, share, half), F32),
             pltpu.VMEM((teams, share, half), F32),
             pltpu.VMEM((chips, share, half), F32),
@@ -309,16 +320,16 @@
             pltpu.VMEM((groups, rows, 128), F32),
             pltpu.VMEM((groups, rows, 128), F32),
             pltpu.VMEM((chips + 2, rows, 128), F32),
-            dma((groups,)), dma((groups,)),
+            dma((PARTS * groups,)), dma((PARTS * groups,)),
             dma((teams,)), dma((teams,)),
             dma((chips,)), dma((chips,)),
             dma((teams,)), dma((teams,)),
-            dma((groups,)), dma((groups,)),
+            dma((PARTS * groups,)), dma((PARTS * groups,)),
             dma((chips,)), dma((chips,)),
-            dma((groups,)), dma((3,)),
+            dma((3,)),
         ],
         compiler_params=pltpu.CompilerParams(
-            collective_id=0, has_side_effects=True, vmem_limit_bytes=48 * 2**20
+            collective_id=0, has_side_effects=True, vmem_limit_bytes=56 * 2**20
         ),
         cost_estimate=pl.CostEstimate(
             flops=4 * members * members * cols, bytes_accessed=8 * rows * points, transcendentals=0

time: 94.2 us -> 85.1 us (0.903)
  local copies, waits for them, and re-layouts: 6.97 us -> 2.02 us
  Pallas kernels: 85.3 us -> 82.1 us
    unnamed x5 -> x1, local copies, waits for them, and re-layouts: 6.97 us -> 2.02 us
    pallas_call x1, Pallas kernels: 85.3 us -> 82.1 us  [on_device(): pl.pallas_call(functools.partial(kernel, groups, chips, factor), out_shap...]
where the time goes in v2:
time: 85.1 us; the launch traced here: 84.1 us
  Pallas kernels  82.1 us (96%)
  local copies, waits for them, and re-layouts  2.02 us (2%)
    pallas_call x1, Pallas kernels, on_device(): pl.pallas_call(functools.partial(kernel, groups, chips, factor), out_shap...  82.1 us
    unnamed x1, local copies, waits for them, and re-layouts  2.02 us

profile of v2, /device:TPU:0, one launch (start us, length us, event | category | flops | bytes accessed | tf_op | source)
XLA Modules:
  0.0 84.1 jit_solution(5097336177817748792)
XLA Ops:
  0.0 82.1 %shard_map.28 = f32[32,32768]{1,0:T(8,128)S(1)} custom-call(bf16[32,32768]{1,0:T(8,128)(2,1)} %x_hbm.1, f32[1,32768]{1,0:T(1,128)} %bitcast.1), custom_call_target="tpu_custom_call" | custom-call | flops 1073741824 | bytes 8388608 | tf_op jit(solution)/shard_map/pallas_call | solution.py:302
  82.1 2.0 %copy.4 = f32[32,32768]{1,0:T(8,128)} copy(f32[32,32768]{1,0:T(8,128)S(1)} %shard_map.28) | data formatting | bytes 8388608

commit v3 on v2

--- a/solution.py
+++ b/solution.py
@@ -15,7 +15,9 @@
 SHIFT = 125.0
 LN2 = math.log(2.0)
 CHUNK = 512
-PARTS = 2
+SPREAD = (4, 3, 1)
+RETURN = ((2,), (3, 2, 1))
+TILE = 128
 
 
 def chunk_at(index):
@@ -38,8 +40,8 @@
     rows = own.shape[0]
     cols = gathered.shape[2]
     members = groups * rows
-    width = cols // PARTS
-    steps = width // CHUNK
+    unit = cols // 8
+    steps = unit // CHUNK
 
     def columns(index):
         return pl.ds(pl.multiple_of(index * cols, cols), cols)
@@ -63,6 +65,12 @@
             src_ref=src, dst_ref=dst, send_sem=send, recv_sem=recv,
             device_id=device, device_id_type=MESH,
         )
+
+    barrier = pltpu.get_barrier_semaphore()
+    for d in range(1, teams):
+        pl.semaphore_signal(barrier, inc=1, device_id=team_peer(d)[1], device_id_type=MESH)
+    for d in range(1, chips):
+        pl.semaphore_signal(barrier, inc=1, device_id=chip_peer(d)[1], device_id_type=MESH)
 
     load_analysis = pltpu.make_async_copy(a_hbm, analysis, local_sem.at[0])
     load_analysis.start()
@@ -71,24 +79,22 @@
     keep = pltpu.make_async_copy(x_hbm.at[:, columns(me)], gathered.at[me], local_sem.at[2])
     keep.start()
 
-    barrier = pltpu.get_barrier_semaphore()
-    for d in range(1, teams):
-        pl.semaphore_signal(barrier, inc=1, device_id=team_peer(d)[1], device_id_type=MESH)
-    for d in range(1, chips):
-        pl.semaphore_signal(barrier, inc=1, device_id=chip_peer(d)[1], device_id_type=MESH)
     pl.semaphore_wait(barrier, teams - 1 + chips - 1)
 
     spread = []
-    for part_at in range(PARTS):
+    start = 0
+    for index, eighths in enumerate(SPREAD):
+        width = eighths * unit
         for d in range(1, groups):
             other, device = group_peer(d)
-            src = pl.ds(pl.multiple_of(other * cols + part_at * width, width), width)
+            src = pl.ds(pl.multiple_of(other * cols + start * unit, unit), width)
             copy = remote(
-                x_hbm.at[:, src], gathered.at[me, :, pl.ds(part_at * width, width)],
-                x_send.at[part_at * groups + d], x_recv.at[part_at * groups + d], device,
+                x_hbm.at[:, src], gathered.at[me, :, pl.ds(start * unit, width)],
+                x_send.at[index * groups + d], x_recv.at[index * groups + d], device,
             )
             copy.start()
             spread.append(copy)
+        start += eighths
 
     load_analysis.wait()
     load_own.wait()
@@ -124,12 +130,12 @@
         return 0
 
     products[...] = jnp.zeros_like(products)
-    for part_at in range(PARTS):
-        for copy in spread[part_at * (groups - 1):(part_at + 1) * (groups - 1)]:
+    start = 0
+    for index, eighths in enumerate(SPREAD):
+        for copy in spread[index * (groups - 1):(index + 1) * (groups - 1)]:
             copy.wait_recv()
-        lax.fori_loop(part_at * steps, (part_at + 1) * steps, add_products, 0)
-    for copy in spread:
-        copy.wait_send()
+        lax.fori_loop(start * steps, (start + eighths) * steps, add_products, 0)
+        start += eighths
     cross = products[...]
     row_index = lax.broadcasted_iota(jnp.int32, (members, members), 0)
     col_index = lax.broadcasted_iota(jnp.int32, (members, members), 1)
@@ -148,6 +154,7 @@
         teams // 2, share, half
     )
 
+    pending = list(spread)
     copies = []
     for d in range(1, teams):
         other, device = team_peer(d)
@@ -156,7 +163,8 @@
         copies.append(copy)
     part_in[rank] = part[rank]
     for copy in copies:
-        copy.wait()
+        copy.wait_recv()
+    pending += copies
     chip_in[chip] = jnp.sum(part_in[...], axis=0)
     copies = []
     for d in range(1, chips):
@@ -165,7 +173,8 @@
         copy.start()
         copies.append(copy)
     for copy in copies:
-        copy.wait()
+        copy.wait_recv()
+    pending += copies
     summed[rank] = jnp.sum(chip_in[...], axis=0)
     copies = []
     for d in range(1, teams):
@@ -174,7 +183,8 @@
         copy.start()
         copies.append(copy)
     for copy in copies:
-        copy.wait()
+        copy.wait_recv()
+    pending += copies
 
     off = 1.0 / jnp.sqrt(summed[: teams // 2].reshape(half, half))
     triangles = summed[teams // 2 :].reshape(half, half)
@@ -211,9 +221,23 @@
             square = square + values[:, k * 128:(k + 1) * 128]
         return along, square
 
+    share_rows = rows // 2
+    lane = lax.broadcasted_iota(jnp.int32, (share_rows, TILE), 1)
     returns = []
-    for part_at in range(PARTS):
-        first_step, last_step = part_at * steps, (part_at + 1) * steps
+
+    def give(message, base, size, d):
+        other, device = group_peer(d)
+        at = message * groups + d
+        span = pl.ds(base, size)
+        copy = remote(
+            sent.at[other, :, span], got.at[me, :, span], r_send.at[at], r_recv.at[at], device
+        )
+        copy.start()
+        returns.append(copy)
+
+    start, base, message = 0, 0, 0
+    for parts in RETURN:
+        first_step, last_step = start * steps, (start + sum(parts)) * steps
         zeros = jnp.zeros((members, 128), F32)
         along, square = lax.fori_loop(first_step, last_step, weigh, (zeros, zeros))
         along = jnp.sum(along, axis=1, keepdims=True)
@@ -238,53 +262,87 @@
             top = jnp.max(top, axis=1, keepdims=True)
             scale = jnp.maximum(top * 1.0079, 1e-30).astype(BF16).astype(F32)
             inverse = RANGE / scale
-
-            def code(i, _, other=other, inverse=inverse, part_at=part_at):
-                rest = weighted[other, :, chunk_at(i + part_at * steps)]
-                size = jnp.exp2(jnp.abs(rest) * inverse - SHIFT)
-                sent[part_at, other, :, chunk_at(i)] = jnp.where(rest < 0.0, -size, size).astype(BF16)
-                return 0
-
-            lax.fori_loop(0, steps, code, 0)
-            lane = lax.broadcasted_iota(jnp.int32, (rows, 128), 1)
-            sent[part_at, other, :, width:] = jnp.where(lane < 64, scale, slope).astype(BF16)
-            at = part_at * groups + d
-            copy = remote(
-                sent.at[part_at, other], got.at[part_at, me], r_send.at[at], r_recv.at[at], device
-            )
-            copy.start()
-            returns.append(copy)
+            heads = jnp.where(lane < 32, scale[:share_rows], slope[:share_rows])
+            tails = jnp.where(lane < 96, scale[share_rows:], slope[share_rows:])
+            sent[other, :, base:base + TILE] = jnp.where(lane < 64, heads, tails).astype(BF16)
+            place_at, step_at = base + TILE, first_step
+            for eighths in parts:
+                width = eighths * unit
+
+                def code(i, _, other=other, inverse=inverse, place_at=place_at, step_at=step_at, width=width):
+                    rest = weighted[other, :, chunk_at(i + step_at)]
+                    size = jnp.exp2(jnp.abs(rest) * inverse - SHIFT)
+                    coded = jnp.where(rest < 0.0, -size, size).astype(BF16)
+                    early = pl.ds(pl.multiple_of(place_at + i * CHUNK, 128), CHUNK)
+                    late = pl.ds(pl.multiple_of(place_at + width + i * CHUNK, 128), CHUNK)
+                    sent[other, :, early] = coded[:share_rows]
+                    sent[other, :, late] = coded[share_rows:]
+                    return 0
+
+                lax.fori_loop(0, eighths * steps, code, 0)
+                place_at, step_at = place_at + 2 * width, step_at + eighths * steps
+            give(message, base, TILE + 2 * parts[0] * unit, d)
+        base += TILE + 2 * parts[0] * unit
+        message += 1
+        for eighths in parts[1:]:
+            for d in range(1, groups):
+                give(message, base, 2 * eighths * unit, d)
+            base += 2 * eighths * unit
+            message += 1
+        start += sum(parts)
 
     for copy in obs_copies:
         copy.wait()
     obs = jnp.sqrt(jnp.sum(jnp.sum(obs_in[:chips], axis=0), axis=1, keepdims=True))
     near = factor / obs
+    share_factor = factor / members
     row_total = totals[me][:, :1]
 
     def finish(piece, offset, count, along_own, value_at):
         def one(i, _):
             point = pl.ds(pl.multiple_of(piece * cols + offset + i * CHUNK, CHUNK), CHUNK)
-            values = own[:, point].astype(F32)
-            spread_term = value_at(chunk_at(i)) - along_own * values
-            out[:, point] = (values - analysis[:, point]) * near + spread_term * (factor / members)
+            out[:, point] = own[:, point].astype(F32) * along_own - analysis[:, point] * near + value_at(i)
             return 0
 
         lax.fori_loop(0, count, one, 0)
 
-    finish(me, 0, cols // CHUNK, row_total, lambda at: weighted[me, :, at])
-    for part_at in range(PARTS):
-        for d in range(1, groups):
-            returns[part_at * (groups - 1) + d - 1].wait()
-            piece = lax.rem(me + groups - d, groups)
-            scale = got[part_at, piece, :, width:width + 1].astype(F32) * (1.0 / (RANGE * LN2))
-            slope = got[part_at, piece, :, width + 64:width + 65].astype(F32)
-
-            def decode(at, piece=piece, scale=scale, part_at=part_at):
-                coded = got[part_at, piece, :, at].astype(F32)
-                size = (jnp.log(jnp.abs(coded)) + SHIFT * LN2) * scale
-                return jnp.where(coded < 0.0, -size, size)
-
-            finish(piece, part_at * width, steps, row_total - slope, decode)
+    finish(
+        me, 0, cols // CHUNK, near - row_total * share_factor,
+        lambda i: weighted[me, :, chunk_at(i)] * share_factor,
+    )
+    start, base, message = 0, 0, 0
+    for parts in RETURN:
+        tile_at = base
+        base += TILE
+        for eighths in parts:
+            width = eighths * unit
+            for d in range(1, groups):
+                copy = returns[message * (groups - 1) + d - 1]
+                copy.wait_recv()
+                pending.append(copy)
+                piece = lax.rem(me + groups - d, groups)
+                tile = got[piece, :, tile_at:tile_at + TILE].astype(F32)
+                scale = jnp.concatenate([tile[:, :1], tile[:, 64:65]], axis=0)
+                scale = scale * (share_factor / (RANGE * LN2))
+                slope = jnp.concatenate([tile[:, 32:33], tile[:, 96:97]], axis=0)
+
+                def decode(i, piece=piece, scale=scale, base=base, width=width):
+                    early = pl.ds(pl.multiple_of(base + i * CHUNK, 128), CHUNK)
+                    late = pl.ds(pl.multiple_of(base + width + i * CHUNK, 128), CHUNK)
+                    coded = jnp.concatenate([got[piece, :, early], got[piece, :, late]], axis=0)
+                    coded = coded.astype(F32)
+                    size = (jnp.log(jnp.abs(coded)) + SHIFT * LN2) * scale
+                    return jnp.where(coded < 0.0, -size, size)
+
+                finish(
+                    piece, start * unit, eighths * steps,
+                    near - (row_total - slope) * share_factor, decode,
+                )
+            base += 2 * width
+            start += eighths
+            message += 1
+    for copy in pending:
+        copy.wait_send()
 
 
 def on_device(ensemble, analysis):
@@ -298,6 +356,7 @@
     half = members // 2
     share = members // teams
     factor = math.sqrt(points * places)
+    messages = sum(len(parts) for parts in RETURN)
     dma = pltpu.SemaphoreType.DMA
     return pl.pallas_call(
         functools.partial(kernel, groups, chips, factor),
@@ -309,8 +368,8 @@
             pltpu.VMEM((rows, points), BF16),
             pltpu.VMEM((1, points), F32),
             pltpu.VMEM((groups, rows, cols), F32),
-            pltpu.VMEM((PARTS, groups, rows, cols // PARTS + 128), BF16),
-            pltpu.VMEM((PARTS, groups, rows, cols // PARTS + 128), BF16),
+            pltpu.VMEM((groups, rows // 2, 2 * cols + len(RETURN) * TILE), BF16),
+            pltpu.VMEM((groups, rows // 2, 2 * cols + len(RETURN) * TILE), BF16),
             pltpu.VMEM((members, members), F32),
             pltpu.VMEM((teams, share, half), F32),
             pltpu.VMEM((teams, share, half), F32),
@@ -320,11 +379,11 @@
             pltpu.VMEM((groups, rows, 128), F32),
             pltpu.VMEM((groups, rows, 128), F32),
             pltpu.VMEM((chips + 2, rows, 128), F32),
-            dma((PARTS * groups,)), dma((PARTS * groups,)),
+            dma((len(SPREAD) * groups,)), dma((len(SPREAD) * groups,)),
             dma((teams,)), dma((teams,)),
             dma((chips,)), dma((chips,)),
             dma((teams,)), dma((teams,)),
-            dma((PARTS * groups,)), dma((PARTS * groups,)),
+            dma((messages * groups,)), dma((messages * groups,)),
             dma((chips,)), dma((chips,)),
             dma((3,)),
         ],

time: 85.1 us -> 81.6 us (0.959); the launches traced: 84.1 us -> 81.5 us
  Pallas kernels: 82.1 us -> 79.5 us
    pallas_call x1, Pallas kernels: 82.1 us -> 79.5 us  [on_device(): pl.pallas_call(functools.partial(kernel, groups, chips, factor), out_shap...]
where the time goes in v3:
time: 81.6 us; the launch traced here: 81.5 us
  Pallas kernels  79.5 us (97%)
  local copies, waits for them, and re-layouts  2.02 us (2%)
    pallas_call x1, Pallas kernels, on_device(): pl.pallas_call(functools.partial(kernel, groups, chips, factor), out_shap...  79.5 us
    unnamed x1, local copies, waits for them, and re-layouts  2.02 us

profile of v3, /device:TPU:0, one launch (start us, length us, event | category | flops | bytes accessed | tf_op | source)
XLA Modules:
  0.0 81.5 jit_solution(10646493635579551287)
XLA Ops:
  0.0 79.5 %shard_map.28 = f32[32,32768]{1,0:T(8,128)S(1)} custom-call(bf16[32,32768]{1,0:T(8,128)(2,1)} %x_hbm.1, f32[1,32768]{1,0:T(1,128)} %bitcast.1), custom_call_target="tpu_custom_call" | custom-call | flops 1073741824 | bytes 8388608 | tf_op jit(solution)/shard_map/pallas_call | solution.py:361
  79.5 2.0 %copy.4 = f32[32,32768]{1,0:T(8,128)} copy(f32[32,32768]{1,0:T(8,128)S(1)} %shard_map.28) | data formatting | bytes 8388608

commit v4 on v3

v4 whole, which is shorter than its diff:
```python
import functools
import math

import jax
import jax.numpy as jnp
from jax import lax
from jax.experimental import pallas as pl
from jax.experimental.pallas import tpu as pltpu
from jax.sharding import PartitionSpec as P

MESH = pl.DeviceIdType.MESH
F32 = jnp.float32
BF16 = jnp.bfloat16
RANGE = 250.0
SHIFT = 125.0
LN2 = math.log(2.0)
CHUNK = 512
SPREAD = (2, 2, 2, 2)
RETURN = ((1,), (2, 2, 2, 1))
TILE = 128


def chunk_at(index):
    return pl.ds(pl.multiple_of(index * CHUNK, CHUNK), CHUNK)


def wide(tile):
    return jnp.concatenate([tile] * (CHUNK // 128), axis=1)


def kernel(
    groups, chips, factor, x_hbm, a_hbm, out,
    gathered, own, analysis, weighted, sent, got,
    products, part, part_in, chip_in, summed, low, totals, lines, inverses, obs_in,
    x_send, x_recv, p_send, p_recv, c_send, c_recv, s_send, s_recv, r_send, r_recv,
    o_send, o_recv, local_sem,
):
    me = lax.axis_index("member")
    place = lax.axis_index("space")
    core = lax.rem(place, 2)
    chip = place // 2
    rank = me * 2 + core
    teams = groups * 2
    rows = own.shape[0]
    cols = gathered.shape[2]
    members = groups * rows
    unit = cols // 8
    steps = unit // CHUNK

    def each(count, body):
        for d in range(1, count):
            body(d)

    def loop(count, body):
        lax.fori_loop(1, count, lambda d, _: (body(d), 0)[1], 0)

    def columns(index):
        return pl.ds(pl.multiple_of(index * cols, cols), cols)

    def group_peer(d):
        other = lax.rem(me // 2 + 2 * groups - d, groups // 2) * 2 + lax.rem(me + (groups - d) // (groups // 2), 2)
        return other, (other, place)

    def group_source(d):
        return lax.rem(me // 2 + d, groups // 2) * 2 + lax.rem(me + (groups - d) // (groups // 2), 2)

    def team_peer(d):
        other = lax.rem(rank + d, teams)
        return other, (other // 2, chip * 2 + lax.rem(other, 2))

    def chip_peer(d):
        other = lax.rem(chip + d, chips)
        return other, (me, other * 2 + core)

    sibling = (me, chip * 2 + 1 - core)

    def remote(src, dst, send, recv, device):
        return pltpu.make_async_remote_copy(
            src_ref=src, dst_ref=dst, send_sem=send, recv_sem=recv,
            device_id=device, device_id_type=MESH,
        )

    barrier = pltpu.get_barrier_semaphore()

    def greet(device):
        pl.semaphore_signal(barrier, inc=1, device_id=device, device_id_type=MESH)

    each(teams, lambda d: greet(team_peer(d)[1]))
    each(chips, lambda d: greet(chip_peer(d)[1]))

    load_analysis = pltpu.make_async_copy(a_hbm, analysis, local_sem.at[0])
    load_analysis.start()
    load_own = pltpu.make_async_copy(x_hbm, own, local_sem.at[1])
    load_own.start()
    keep = pltpu.make_async_copy(x_hbm.at[:, columns(me)], gathered.at[me], local_sem.at[2])
    keep.start()

    pl.semaphore_wait(barrier, teams - 1 + chips - 1)

    def spread(index, start, d):
        width = SPREAD[index] * unit
        other, device = group_peer(d)
        src = pl.ds(pl.multiple_of(other * cols + start * unit, unit), width)
        at = index * groups + d
        return remote(
            x_hbm.at[:, src], gathered.at[me, :, pl.ds(start * unit, width)],
            x_send.at[at], x_recv.at[at], device,
        )

    start = 0
    for index, eighths in enumerate(SPREAD):
        each(groups, lambda d: spread(index, start, d).start())
        start += eighths

    load_analysis.wait()
    load_own.wait()

    def add_distance(i, total):
        at = chunk_at(i)
        deviation = own[:, at].astype(F32) - analysis[:, at]
        square = deviation * deviation
        for k in range(CHUNK // 128):
            total = total + square[:, k * 128:(k + 1) * 128]
        return total

    distance = lax.fori_loop(0, own.shape[1] // CHUNK, add_distance, jnp.zeros((rows, 128), F32))
    obs_in[chips] = distance
    pair = remote(obs_in.at[chips], obs_in.at[chips + 1], o_send.at[0], o_recv.at[0], sibling)
    pair.start()
    pair.wait()
    obs_in[chip] = distance + obs_in[chips + 1]

    def obs_copy(d):
        return remote(
            obs_in.at[chip], obs_in.at[chip], o_send.at[d], o_recv.at[d], chip_peer(d)[1]
        )

    each(chips, lambda d: obs_copy(d).start())
    keep.wait()

    def add_products(i, _):
        block = gathered[:, :, chunk_at(i)].reshape(members, CHUNK)
        products[...] += lax.dot_general(
            block, block, (((1,), (1,)), ((), ())), preferred_element_type=F32
        )
        return 0

    products[...] = jnp.zeros_like(products)
    start = 0
    for index, eighths in enumerate(SPREAD):
        each(groups, lambda d: spread(index, start, d).wait_recv())
        lax.fori_loop(start * steps, (start + eighths) * steps, add_products, 0)
        start += eighths
    cross = products[...]
    row_index = lax.broadcasted_iota(jnp.int32, (members, members), 0)
    col_index = lax.broadcasted_iota(jnp.int32, (members, members), 1)
    diagonal = jnp.where(row_index == col_index, cross, 0.0)
    norm_rows = jnp.sum(diagonal, axis=1, keepdims=True)
    norm_cols = jnp.sum(diagonal, axis=0, keepdims=True)
    pair_sq = norm_rows + norm_cols - 2.0 * cross
    half = members // 2
    small_row = lax.broadcasted_iota(jnp.int32, (half, half), 0)
    small_col = lax.broadcasted_iota(jnp.int32, (half, half), 1)
    upper = small_col > small_row
    lower = small_col < small_row
    share = members // teams
    part[: teams // 2] = pair_sq[:half, half:].reshape(teams // 2, share, half)
    part[teams // 2 :] = jnp.where(upper, pair_sq[:half, :half], pair_sq[half:, half:]).reshape(
        teams // 2, share, half
    )

    def part_copy(d):
        other, device = team_peer(d)
        return remote(part.at[other], part_in.at[rank], p_send.at[d], p_recv.at[d], device)

    def chip_copy(d):
        return remote(
            chip_in.at[chip], chip_in.at[chip], c_send.at[d], c_recv.at[d], chip_peer(d)[1]
        )

    def sum_copy(d):
        return remote(
            summed.at[rank], summed.at[rank], s_send.at[d], s_recv.at[d], team_peer(d)[1]
        )

    each(teams, lambda d: part_copy(d).start())
    part_in[rank] = part[rank]
    each(teams, lambda d: part_copy(d).wait_recv())
    chip_in[chip] = jnp.sum(part_in[...], axis=0)
    each(chips, lambda d: chip_copy(d).start())
    each(chips, lambda d: chip_copy(d).wait_recv())
    summed[rank] = jnp.sum(chip_in[...], axis=0)
    each(teams, lambda d: sum_copy(d).start())
    each(teams, lambda d: sum_copy(d).wait_recv())

    off = 1.0 / jnp.sqrt(summed[: teams // 2].reshape(half, half))
    triangles = summed[teams // 2 :].reshape(half, half)
    triangles = jnp.where(small_row == small_col, 1.0, triangles)
    triangles = 1.0 / jnp.sqrt(triangles)
    above = jnp.where(upper, triangles, 0.0)
    below = jnp.where(lower, triangles, 0.0)
    first = above + above.T
    second = below + below.T
    off_t = off.T
    def slope_of(own_part, own_products, cross_part, cross_products):
        along = jnp.sum(own_part * own_products + cross_part * cross_products, axis=1, keepdims=True)
        square = jnp.sum(jnp.where(small_row == small_col, own_products, 0.0), axis=1, keepdims=True)
        slope = jnp.where(square > 0.0, along / jnp.where(square > 0.0, square, 1.0), 0.0)
        return slope.astype(BF16).astype(F32)

    slope_first = slope_of(first, products[:half, :half], off, products[:half, half:])
    slope_second = slope_of(second, products[half:, half:], off_t, products[half:, :half])
    low[:half, :half] = jnp.where(small_row == small_col, -slope_first, first).astype(BF16)
    low[:half, half:] = off.astype(BF16)
    low[half:, :half] = off_t.astype(BF16)
    low[half:, half:] = jnp.where(small_row == small_col, -slope_second, second).astype(BF16)
    slopes = jnp.concatenate([slope_first, slope_second], axis=0)
    slopes = jnp.broadcast_to(slopes, (members, 128)).reshape(groups, rows, 128)
    lines[...] = slopes
    total_first = jnp.sum(first + off, axis=1, keepdims=True)
    total_second = jnp.sum(second + off_t, axis=1, keepdims=True)
    groups_half = groups // 2
    totals[:groups_half] = jnp.broadcast_to(total_first, (half, 128)).reshape(groups_half, rows, 128)
    totals[groups_half:] = jnp.broadcast_to(total_second, (half, 128)).reshape(
        groups_half, rows, 128
    )

    def weigh(i, top):
        at = chunk_at(i)
        block = gathered[:, :, at].reshape(members, CHUNK)
        rest = jnp.dot(low[...], block, preferred_element_type=F32)
        weighted[:, :, at] = rest.reshape(groups, rows, CHUNK)
        rest = jnp.abs(rest)
        for k in range(CHUNK // 128):
            top = jnp.maximum(top, rest[:, k * 128:(k + 1) * 128])
        return top

    share_rows = rows // 2
    lane = lax.broadcasted_iota(jnp.int32, (groups, share_rows, TILE), 2)

    def give(message, base, size, d):
        other, device = group_peer(d)
        at = message * groups + d
        span = pl.ds(base, size)
        return remote(
            sent.at[other, :, span], got.at[me, :, span], r_send.at[at], r_recv.at[at], device
        )

    sizes = []
    start, base, message = 0, 0, 0
    for parts in RETURN:
        first_step, last_step = start * steps, (start + sum(parts)) * steps
        top = lax.fori_loop(first_step, last_step, weigh, jnp.zeros((members, 128), F32))
        top = jnp.max(top, axis=1, keepdims=True)
        scale = jnp.maximum(top * 1.0079, 1e-30).astype(BF16).astype(F32)
        scale = jnp.broadcast_to(scale, (members, 128)).reshape(groups, rows, 128)
        inverses[...] = RANGE / scale
        heads = jnp.where(lane < 32, scale[:, :share_rows], slopes[:, :share_rows])
        tails = jnp.where(lane < 96, scale[:, share_rows:], slopes[:, share_rows:])
        sent[:, :, base:base + TILE] = jnp.where(lane < 64, heads, tails).astype(BF16)
        first_size = TILE + 2 * parts[0] * unit

        def encode(d):
            other = group_peer(d)[0]
            inverse = inverses[other]
            place_at, step_at = base + TILE, first_step
            for eighths in parts:
                width = eighths * unit

                def code(i, _, place_at=place_at, step_at=step_at, width=width):
                    rest = weighted[other, :, chunk_at(i + step_at)]
                    size = jnp.exp2(jnp.abs(rest) * wide(inverse) - SHIFT)
                    coded = jnp.where(rest < 0.0, -size, size).astype(BF16)
                    early = pl.ds(pl.multiple_of(place_at + i * CHUNK, 128), CHUNK)
                    late = pl.ds(pl.multiple_of(place_at + width + i * CHUNK, 128), CHUNK)
                    sent[other, :, early] = coded[:share_rows]
                    sent[other, :, late] = coded[share_rows:]
                    return 0

                lax.fori_loop(0, eighths * steps, code, 0)
                place_at, step_at = place_at + 2 * width, step_at + eighths * steps
            give(message, base, first_size, d).start()

        loop(groups, encode)
        sizes.append((base, first_size))
        base += first_size
        message += 1
        for eighths in parts[1:]:
            size = 2 * eighths * unit
            each(groups, lambda d: give(message, base, size, d).start())
            sizes.append((base, size))
            base += size
            message += 1
        start += sum(parts)

    each(chips, lambda d: obs_copy(d).wait_recv())
    obs = jnp.sqrt(jnp.sum(jnp.sum(obs_in[:chips], axis=0), axis=1, keepdims=True))
    near = jnp.broadcast_to(factor / obs, (rows, 128))
    share_factor = factor / members
    row_total = totals[me]

    def finish(piece, offset, count, along_own, value_at):
        def one(i, _):
            point = pl.ds(pl.multiple_of(piece * cols + offset + i * CHUNK, CHUNK), CHUNK)
            ours = own[:, point].astype(F32) * wide(along_own)
            out[:, point] = ours - analysis[:, point] * wide(near) + value_at(i)
            return 0

        lax.fori_loop(0, count, one, 0)

    finish(
        me, 0, cols // CHUNK, near - (row_total - lines[me]) * share_factor,
        lambda i: weighted[me, :, chunk_at(i)] * share_factor,
    )
    start, base, message = 0, 0, 0
    for parts in RETURN:
        tile_at = base
        base += TILE
        for eighths in parts:
            width = eighths * unit
            def take(d):
                give(message, *sizes[message], d).wait_recv()
                piece = group_source(d)
                tile = got[piece, :, tile_at:tile_at + TILE].astype(F32)
                scale = jnp.concatenate([tile[:, :1], tile[:, 64:65]], axis=0)
                scale = jnp.broadcast_to(scale * (share_factor / (RANGE * LN2)), (rows, 128))
                slope = jnp.concatenate([tile[:, 32:33], tile[:, 96:97]], axis=0)
                slope = jnp.broadcast_to(slope, (rows, 128))

                def decode(i):
                    early = pl.ds(pl.multiple_of(base + i * CHUNK, 128), CHUNK)
                    late = pl.ds(pl.multiple_of(base + width + i * CHUNK, 128), CHUNK)
                    coded = jnp.concatenate([got[piece, :, early], got[piece, :, late]], axis=0)
                    coded = coded.astype(F32)
                    size = (jnp.log(jnp.abs(coded)) + SHIFT * LN2) * wide(scale)
                    return jnp.where(coded < 0.0, -size, size)

                finish(
                    piece, start * unit, eighths * steps,
                    near - (row_total - slope) * share_factor, decode,
                )

            loop(groups, take)
            base += 2 * width
            start += eighths
            message += 1

    start = 0
    for index, eighths in enumerate(SPREAD):
        each(groups, lambda d: spread(index, start, d).wait_send())
        start += eighths
    each(chips, lambda d: obs_copy(d).wait_send())
    each(teams, lambda d: part_copy(d).wait_send())
    each(chips, lambda d: chip_copy(d).wait_send())
    each(teams, lambda d: sum_copy(d).wait_send())
    for message, (base, size) in enumerate(sizes):
        each(groups, lambda d: give(message, base, size, d).wait_send())


def on_device(ensemble, analysis):
    rows, points = ensemble.shape
    groups = lax.axis_size("member")
    places = lax.axis_size("space")
    chips = places // 2
    teams = groups * 2
    members = rows * groups
    cols = points // groups
    half = members // 2
    share = members // teams
    factor = math.sqrt(points * places)
    messages = sum(len(parts) for parts in RETURN)
    dma = pltpu.SemaphoreType.DMA
    return pl.pallas_call(
        functools.partial(kernel, groups, chips, factor),
        out_shape=pltpu.VMEM((rows, points), F32),
        in_specs=[pl.BlockSpec(memory_space=pltpu.HBM)] * 2,
        out_specs=pl.BlockSpec(memory_space=pltpu.VMEM),
        scratch_shapes=[
            pltpu.VMEM((groups, rows, cols), BF16),
            pltpu.VMEM((rows, points), BF16),
            pltpu.VMEM((1, points), F32),
            pltpu.VMEM((groups, rows, cols), F32),
            pltpu.VMEM((groups, rows // 2, 2 * cols + len(RETURN) * TILE), BF16),
            pltpu.VMEM((groups, rows // 2, 2 * cols + len(RETURN) * TILE), BF16),
            pltpu.VMEM((members, members), F32),
            pltpu.VMEM((teams, share, half), F32),
            pltpu.VMEM((teams, share, half), F32),
            pltpu.VMEM((chips, share, half), F32),
            pltpu.VMEM((teams, share, half), F32),
            pltpu.VMEM((members, members), BF16),
            pltpu.VMEM((groups, rows, 128), F32),
            pltpu.VMEM((groups, rows, 128), F32),
            pltpu.VMEM((groups, rows, 128), F32),
            pltpu.VMEM((chips + 2, rows, 128), F32),
            dma((len(SPREAD) * groups,)), dma((len(SPREAD) * groups,)),
            dma((teams,)), dma((teams,)),
            dma((chips,)), dma((chips,)),
            dma((teams,)), dma((teams,)),
            dma((messages * groups,)), dma((messages * groups,)),
            dma((chips,)), dma((chips,)),
            dma((3,)),
        ],
        compiler_params=pltpu.CompilerParams(
            collective_id=0, has_side_effects=True, vmem_limit_bytes=56 * 2**20
        ),
        cost_estimate=pl.CostEstimate(
            flops=4 * members * members * cols, bytes_accessed=8 * rows * points, transcendentals=0
        ),
    )(ensemble, analysis.reshape(1, points))


def solution(mesh):
    placed = (P("member", "space"), P("space"))
    return jax.shard_map(
        on_device, mesh=mesh, in_specs=placed, out_specs=P("member", "space"), check_vma=False
    )
```

time: 81.6 us -> 79 us (0.968)
  Pallas kernels: 79.5 us -> 76.7 us
    pallas_call x1, Pallas kernels: 79.5 us -> 76.7 us  [on_device(): pl.pallas_call(functools.partial(kernel, groups, chips, factor), out_shap...]
where the time goes in v4:
time: 79 us; the launch traced here: 78.8 us
  Pallas kernels  76.7 us (97%)
  local copies, waits for them, and re-layouts  2.02 us (3%)
    pallas_call x1, Pallas kernels, on_device(): pl.pallas_call(functools.partial(kernel, groups, chips, factor), out_shap...  76.7 us
    unnamed x1, local copies, waits for them, and re-layouts  2.02 us

profile of v4, /device:TPU:0, one launch (start us, length us, event | category | flops | bytes accessed | tf_op | source)
XLA Modules:
  0.0 78.8 jit_solution(348596260783982029)
XLA Ops:
  0.0 76.7 %shard_map.28 = f32[32,32768]{1,0:T(8,128)S(1)} custom-call(bf16[32,32768]{1,0:T(8,128)(2,1)} %x_hbm.1, f32[1,32768]{1,0:T(1,128)} %bitcast.1), custom_call_target="tpu_custom_call" | custom-call | flops 1073741824 | bytes 8388608 | tf_op jit(solution)/shard_map/pallas_call | solution.py:373
  76.8 2.0 %copy.4 = f32[32,32768]{1,0:T(8,128)} copy(f32[32,32768]{1,0:T(8,128)S(1)} %shard_map.28) | data formatting | bytes 8388608

commit v5 on v4

--- a/solution.py
+++ b/solution.py
@@ -11,8 +11,7 @@
 MESH = pl.DeviceIdType.MESH
 F32 = jnp.float32
 BF16 = jnp.bfloat16
-RANGE = 250.0
-SHIFT = 125.0
+RANGE = 125.0
 LN2 = math.log(2.0)
 CHUNK = 512
 SPREAD = (2, 2, 2, 2)
@@ -85,7 +84,8 @@
     def greet(device):
         pl.semaphore_signal(barrier, inc=1, device_id=device, device_id_type=MESH)
 
-    each(teams, lambda d: greet(team_peer(d)[1]))
+    greet(sibling)
+    each(groups, lambda d: greet(group_peer(d)[1]))
     each(chips, lambda d: greet(chip_peer(d)[1]))
 
     load_analysis = pltpu.make_async_copy(a_hbm, analysis, local_sem.at[0])
@@ -95,7 +95,7 @@
     keep = pltpu.make_async_copy(x_hbm.at[:, columns(me)], gathered.at[me], local_sem.at[2])
     keep.start()
 
-    pl.semaphore_wait(barrier, teams - 1 + chips - 1)
+    pl.semaphore_wait(barrier, groups + chips - 1)
 
     def spread(index, start, d):
         width = SPREAD[index] * unit
@@ -138,18 +138,17 @@
     each(chips, lambda d: obs_copy(d).start())
     keep.wait()
 
-    def add_products(i, _):
-        block = gathered[:, :, chunk_at(i)].reshape(members, CHUNK)
-        products[...] += lax.dot_general(
-            block, block, (((1,), (1,)), ((), ())), preferred_element_type=F32
-        )
-        return 0
-
-    products[...] = jnp.zeros_like(products)
+    def products_of(start, size):
+        block = gathered[:, :, start:start + size].reshape(members, size)
+        return lax.dot_general(block, block, (((1,), (1,)), ((), ())), preferred_element_type=F32)
+
     start = 0
     for index, eighths in enumerate(SPREAD):
         each(groups, lambda d: spread(index, start, d).wait_recv())
-        lax.fori_loop(start * steps, (start + eighths) * steps, add_products, 0)
+        if start:
+            products[...] += products_of(start * unit, eighths * unit)
+        else:
+            products[...] = products_of(0, eighths * unit)
         start += eighths
     cross = products[...]
     row_index = lax.broadcasted_iota(jnp.int32, (members, members), 0)
@@ -269,8 +268,7 @@
 
                 def code(i, _, place_at=place_at, step_at=step_at, width=width):
                     rest = weighted[other, :, chunk_at(i + step_at)]
-                    size = jnp.exp2(jnp.abs(rest) * wide(inverse) - SHIFT)
-                    coded = jnp.where(rest < 0.0, -size, size).astype(BF16)
+                    coded = jnp.exp2(rest * wide(inverse)).astype(BF16)
                     early = pl.ds(pl.multiple_of(place_at + i * CHUNK, 128), CHUNK)
                     late = pl.ds(pl.multiple_of(place_at + width + i * CHUNK, 128), CHUNK)
                     sent[other, :, early] = coded[:share_rows]
@@ -331,9 +329,7 @@
                     early = pl.ds(pl.multiple_of(base + i * CHUNK, 128), CHUNK)
                     late = pl.ds(pl.multiple_of(base + width + i * CHUNK, 128), CHUNK)
                     coded = jnp.concatenate([got[piece, :, early], got[piece, :, late]], axis=0)
-                    coded = coded.astype(F32)
-                    size = (jnp.log(jnp.abs(coded)) + SHIFT * LN2) * wide(scale)
-                    return jnp.where(coded < 0.0, -size, size)
+                    return jnp.log(coded.astype(F32)) * wide(scale)
 
                 finish(
                     piece, start * unit, eighths * steps,

time: 79 us -> 78.4 us (level)
  no operation moved by 1% of the time
where the time goes in v5:
time: 78.4 us; the launch traced here: 78.2 us
  Pallas kernels  76.2 us (97%)
  local copies, waits for them, and re-layouts  2.02 us (3%)
    pallas_call x1, Pallas kernels, on_device(): pl.pallas_call(functools.partial(kernel, groups, chips, factor), out_shap...  76.2 us
    unnamed x1, local copies, waits for them, and re-layouts  2.02 us

profile of v5, /device:TPU:0, one launch (start us, length us, event | category | flops | bytes accessed | tf_op | source)
XLA Modules:
  0.0 78.2 jit_solution(14598341301670296669)
XLA Ops:
  0.0 76.2 %shard_map.28 = f32[32,32768]{1,0:T(8,128)S(1)} custom-call(bf16[32,32768]{1,0:T(8,128)(2,1)} %x_hbm.1, f32[1,32768]{1,0:T(1,128)} %bitcast.1), custom_call_target="tpu_custom_call" | custom-call | flops 1073741824 | bytes 8388608 | tf_op jit(solution)/shard_map/pallas_call | solution.py:369
  76.2 2.0 %copy.4 = f32[32,32768]{1,0:T(8,128)} copy(f32[32,32768]{1,0:T(8,128)S(1)} %shard_map.28) | data formatting | bytes 8388608

commit v6 on v5

--- a/solution.py
+++ b/solution.py
@@ -17,6 +17,8 @@
 SPREAD = (2, 2, 2, 2)
 RETURN = ((1,), (2, 2, 2, 1))
 TILE = 128
+CHIP_STEPS = ((2, 1), (1, 1), (3, 1), (2, 0), (0, 1), (1, 0), (3, 0))
+STEPS = ((2, 1), (2, 0), (3, 1), (1, 1), (0, 1), (3, 0), (1, 0))
 
 
 def chunk_at(index):
@@ -50,25 +52,26 @@
         for d in range(1, count):
             body(d)
 
-    def loop(count, body):
-        lax.fori_loop(1, count, lambda d, _: (body(d), 0)[1], 0)
-
     def columns(index):
         return pl.ds(pl.multiple_of(index * cols, cols), cols)
 
     def group_peer(d):
-        other = lax.rem(me // 2 + 2 * groups - d, groups // 2) * 2 + lax.rem(me + (groups - d) // (groups // 2), 2)
+        dz, dy = STEPS[d - 1]
+        other = lax.rem(me // 2 + dz, groups // 2) * 2 + lax.rem(me + dy, 2)
         return other, (other, place)
 
     def group_source(d):
-        return lax.rem(me // 2 + d, groups // 2) * 2 + lax.rem(me + (groups - d) // (groups // 2), 2)
+        dz, dy = STEPS[d - 1]
+        return lax.rem(me // 2 + groups // 2 - dz, groups // 2) * 2 + lax.rem(me + dy, 2)
 
     def team_peer(d):
-        other = lax.rem(rank + d, teams)
-        return other, (other // 2, chip * 2 + lax.rem(other, 2))
+        member = group_peer((d + 1) // 2)[0] if d < teams - 1 else me
+        its_core = core if d % 2 == 0 else 1 - core
+        return member * 2 + its_core, (member, chip * 2 + its_core)
 
     def chip_peer(d):
-        other = lax.rem(chip + d, chips)
+        dx, dy = CHIP_STEPS[d - 1]
+        other = lax.rem(chip // 2 + dx, chips // 2) * 2 + lax.rem(chip + dy, 2)
         return other, (me, other * 2 + core)
 
     sibling = (me, chip * 2 + 1 - core)
@@ -279,7 +282,7 @@
                 place_at, step_at = place_at + 2 * width, step_at + eighths * steps
             give(message, base, first_size, d).start()
 
-        loop(groups, encode)
+        each(groups, encode)
         sizes.append((base, first_size))
         base += first_size
         message += 1
@@ -336,7 +339,7 @@
                     near - (row_total - slope) * share_factor, decode,
                 )
 
-            loop(groups, take)
+            each(groups, take)
             base += 2 * width
             start += eighths
             message += 1

time: 78.4 us -> 77.5 us (0.989)
  Pallas kernels: 76.2 us -> 75.3 us
    pallas_call x1, Pallas kernels: 76.2 us -> 75.3 us  [on_device(): pl.pallas_call(functools.partial(kernel, groups, chips, factor), out_shap...]
where the time goes in v6:
time: 77.5 us; the launch traced here: 77.4 us
  Pallas kernels  75.3 us (97%)
  local copies, waits for them, and re-layouts  2.02 us (3%)
    pallas_call x1, Pallas kernels, on_device(): pl.pallas_call(functools.partial(kernel, groups, chips, factor), out_shap...  75.3 us
    unnamed x1, local copies, waits for them, and re-layouts  2.02 us

profile of v6, /device:TPU:0, one launch (start us, length us, event | category | flops | bytes accessed | tf_op | source)
XLA Modules:
  0.0 77.4 jit_solution(5399466917735988365)
XLA Ops:
  0.0 75.3 %shard_map.28 = f32[32,32768]{1,0:T(8,128)S(1)} custom-call(bf16[32,32768]{1,0:T(8,128)(2,1)} %x_hbm.1, f32[1,32768]{1,0:T(1,128)} %bitcast.1), custom_call_target="tpu_custom_call" | custom-call | flops 1073741824 | bytes 8388608 | tf_op jit(solution)/shard_map/pallas_call | solution.py:372
  75.3 2.0 %copy.4 = f32[32,32768]{1,0:T(8,128)} copy(f32[32,32768]{1,0:T(8,128)S(1)} %shard_map.28) | data formatting | bytes 8388608

commit v7 on v6

--- a/solution.py
+++ b/solution.py
@@ -14,8 +14,8 @@
 RANGE = 125.0
 LN2 = math.log(2.0)
 CHUNK = 512
-SPREAD = (2, 2, 2, 2)
-RETURN = ((1,), (2, 2, 2, 1))
+SPREAD = (3, 3, 2)
+RETURN = ((1,), (4, 2, 1))
 TILE = 128
 CHIP_STEPS = ((2, 1), (1, 1), (3, 1), (2, 0), (0, 1), (1, 0), (3, 0))
 STEPS = ((2, 1), (2, 0), (3, 1), (1, 1), (0, 1), (3, 0), (1, 0))
@@ -300,7 +300,7 @@
     share_factor = factor / members
     row_total = totals[me]
 
-    def finish(piece, offset, count, along_own, value_at):
+    def fill(piece, offset, count, along_own, value_at):
         def one(i, _):
             point = pl.ds(pl.multiple_of(piece * cols + offset + i * CHUNK, CHUNK), CHUNK)
             ours = own[:, point].astype(F32) * wide(along_own)
@@ -309,7 +309,7 @@
 
         lax.fori_loop(0, count, one, 0)
 
-    finish(
+    fill(
         me, 0, cols // CHUNK, near - (row_total - lines[me]) * share_factor,
         lambda i: weighted[me, :, chunk_at(i)] * share_factor,
     )
@@ -317,26 +317,38 @@
     for parts in RETURN:
         tile_at = base
         base += TILE
-        for eighths in parts:
+        for nth, eighths in enumerate(parts):
             width = eighths * unit
+
             def take(d):
                 give(message, *sizes[message], d).wait_recv()
                 piece = group_source(d)
-                tile = got[piece, :, tile_at:tile_at + TILE].astype(F32)
-                scale = jnp.concatenate([tile[:, :1], tile[:, 64:65]], axis=0)
-                scale = jnp.broadcast_to(scale * (share_factor / (RANGE * LN2)), (rows, 128))
-                slope = jnp.concatenate([tile[:, 32:33], tile[:, 96:97]], axis=0)
-                slope = jnp.broadcast_to(slope, (rows, 128))
-
-                def decode(i):
+
+                def decode(i, scale):
                     early = pl.ds(pl.multiple_of(base + i * CHUNK, 128), CHUNK)
                     late = pl.ds(pl.multiple_of(base + width + i * CHUNK, 128), CHUNK)
                     coded = jnp.concatenate([got[piece, :, early], got[piece, :, late]], axis=0)
                     return jnp.log(coded.astype(F32)) * wide(scale)
 
-                finish(
-                    piece, start * unit, eighths * steps,
-                    near - (row_total - slope) * share_factor, decode,
+                def add(i, _):
+                    point = piece * cols + start * unit + i * CHUNK
+                    point = pl.ds(pl.multiple_of(point, CHUNK), CHUNK)
+                    out[:, point] += decode(i, inverses[piece])
+                    return 0
+
+                if nth:
+                    lax.fori_loop(0, eighths * steps, add, 0)
+                    return
+                tile = got[piece, :, tile_at:tile_at + TILE].astype(F32)
+                scale = jnp.concatenate([tile[:, :1], tile[:, 64:65]], axis=0)
+                scale = jnp.broadcast_to(scale * (share_factor / (RANGE * LN2)), (rows, 128))
+                inverses[piece] = scale
+                slope = jnp.concatenate([tile[:, 32:33], tile[:, 96:97]], axis=0)
+                along_own = near - (row_total - jnp.broadcast_to(slope, (rows, 128))) * share_factor
+                fill(piece, start * unit, eighths * steps, along_own, lambda i: decode(i, scale))
+                fill(
+                    piece, (start + eighths) * unit, sum(parts[1:]) * steps, along_own,
+                    lambda i: 0.0,
                 )
 
             each(groups, take)

time: 77.5 us -> 76.7 us (0.990)
  no operation moved by 1% of the time
where the time goes in v7:
time: 76.7 us; the launch traced here: 76.6 us
  Pallas kernels  74.6 us (97%)
  local copies, waits for them, and re-layouts  2.02 us (3%)
    pallas_call x1, Pallas kernels, on_device(): pl.pallas_call(functools.partial(kernel, groups, chips, factor), out_shap...  74.6 us
    unnamed x1, local copies, waits for them, and re-layouts  2.02 us

profile of v7, /device:TPU:0, one launch (start us, length us, event | category | flops | bytes accessed | tf_op | source)
XLA Modules:
  0.0 76.6 jit_solution(16221662224207376443)
XLA Ops:
  0.0 74.6 %shard_map.28 = f32[32,32768]{1,0:T(8,128)S(1)} custom-call(bf16[32,32768]{1,0:T(8,128)(2,1)} %x_hbm.1, f32[1,32768]{1,0:T(1,128)} %bitcast.1), custom_call_target="tpu_custom_call" | custom-call | flops 1073741824 | bytes 8388608 | tf_op jit(solution)/shard_map/pallas_call | solution.py:384
  74.6 2.0 %copy.4 = f32[32,32768]{1,0:T(8,128)} copy(f32[32,32768]{1,0:T(8,128)S(1)} %shard_map.28) | data formatting | bytes 8388608

commit v8 on v7

--- a/solution.py
+++ b/solution.py
@@ -15,7 +15,7 @@
 LN2 = math.log(2.0)
 CHUNK = 512
 SPREAD = (3, 3, 2)
-RETURN = ((1,), (4, 2, 1))
+RETURN = ((1,), (5, 2))
 TILE = 128
 CHIP_STEPS = ((2, 1), (1, 1), (3, 1), (2, 0), (0, 1), (1, 0), (3, 0))
 STEPS = ((2, 1), (2, 0), (3, 1), (1, 1), (0, 1), (3, 0), (1, 0))
@@ -204,14 +204,13 @@
     first = above + above.T
     second = below + below.T
     off_t = off.T
-    def slope_of(own_part, own_products, cross_part, cross_products):
+    def slope_of(own_part, own_products, cross_part, cross_products, square):
         along = jnp.sum(own_part * own_products + cross_part * cross_products, axis=1, keepdims=True)
-        square = jnp.sum(jnp.where(small_row == small_col, own_products, 0.0), axis=1, keepdims=True)
         slope = jnp.where(square > 0.0, along / jnp.where(square > 0.0, square, 1.0), 0.0)
         return slope.astype(BF16).astype(F32)
 
-    slope_first = slope_of(first, products[:half, :half], off, products[:half, half:])
-    slope_second = slope_of(second, products[half:, half:], off_t, products[half:, :half])
+    slope_first = slope_of(first, products[:half, :half], off, products[:half, half:], norm_rows[:half])
+    slope_second = slope_of(second, products[half:, half:], off_t, products[half:, :half], norm_rows[half:])
     low[:half, :half] = jnp.where(small_row == small_col, -slope_first, first).astype(BF16)
     low[:half, half:] = off.astype(BF16)
     low[half:, :half] = off_t.astype(BF16)
@@ -313,6 +312,14 @@
         me, 0, cols // CHUNK, near - (row_total - lines[me]) * share_factor,
         lambda i: weighted[me, :, chunk_at(i)] * share_factor,
     )
+    start = 0
+    for index, eighths in enumerate(SPREAD):
+        each(groups, lambda d: spread(index, start, d).wait_send())
+        start += eighths
+    each(chips, lambda d: obs_copy(d).wait_send())
+    each(teams, lambda d: part_copy(d).wait_send())
+    each(chips, lambda d: chip_copy(d).wait_send())
+    each(teams, lambda d: sum_copy(d).wait_send())
     start, base, message = 0, 0, 0
     for parts in RETURN:
         tile_at = base
@@ -352,20 +359,13 @@
                 )
 
             each(groups, take)
+            if message:
+                each(groups, lambda d: give(message - 1, *sizes[message - 1], d).wait_send())
             base += 2 * width
             start += eighths
             message += 1
 
-    start = 0
-    for index, eighths in enumerate(SPREAD):
-        each(groups, lambda d: spread(index, start, d).wait_send())
-        start += eighths
-    each(chips, lambda d: obs_copy(d).wait_send())
-    each(teams, lambda d: part_copy(d).wait_send())
-    each(chips, lambda d: chip_copy(d).wait_send())
-    each(teams, lambda d: sum_copy(d).wait_send())
-    for message, (base, size) in enumerate(sizes):
-        each(groups, lambda d: give(message, base, size, d).wait_send())
+    each(groups, lambda d: give(message - 1, *sizes[message - 1], d).wait_send())
 
 
 def on_device(ensemble, analysis):

time: 76.7 us -> 76.6 us (level)
  no operation moved by 1% of the time
where the time goes in v8:
time: 76.6 us; the launch traced here: 76 us
  Pallas kernels  74 us (97%)
  local copies, waits for them, and re-layouts  2.02 us (3%)
    pallas_call x1, Pallas kernels, on_device(): pl.pallas_call(functools.partial(kernel, groups, chips, factor), out_shap...  74 us
    unnamed x1, local copies, waits for them, and re-layouts  2.02 us

profile of v8, /device:TPU:0, one launch (start us, length us, event | category | flops | bytes accessed | tf_op | source)
XLA Modules:
  0.0 76.0 jit_solution(11012083543964111941)
XLA Ops:
  0.0 74.0 %shard_map.28 = f32[32,32768]{1,0:T(8,128)S(1)} custom-call(bf16[32,32768]{1,0:T(8,128)(2,1)} %x_hbm.1, f32[1,32768]{1,0:T(1,128)} %bitcast.1), custom_call_target="tpu_custom_call" | custom-call | flops 1073741824 | bytes 8388608 | tf_op jit(solution)/shard_map/pallas_call | solution.py:384
  74.0 2.0 %copy.4 = f32[32,32768]{1,0:T(8,128)} copy(f32[32,32768]{1,0:T(8,128)S(1)} %shard_map.28) | data formatting | bytes 8388608

commit v9 on v8

--- a/solution.py
+++ b/solution.py
@@ -15,7 +15,7 @@
 LN2 = math.log(2.0)
 CHUNK = 512
 SPREAD = (3, 3, 2)
-RETURN = ((1,), (5, 2))
+RETURN = ((1,), (6, 1))
 TILE = 128
 CHIP_STEPS = ((2, 1), (1, 1), (3, 1), (2, 0), (0, 1), (1, 0), (3, 0))
 STEPS = ((2, 1), (2, 0), (3, 1), (1, 1), (0, 1), (3, 0), (1, 0))
@@ -65,8 +65,9 @@
         return lax.rem(me // 2 + groups // 2 - dz, groups // 2) * 2 + lax.rem(me + dy, 2)
 
     def team_peer(d):
-        member = group_peer((d + 1) // 2)[0] if d < teams - 1 else me
-        its_core = core if d % 2 == 0 else 1 - core
+        nth = (d - 1) % (groups - 1) + 1
+        member = group_peer(nth)[0] if d < teams - 1 else me
+        its_core = core if d < groups else 1 - core
         return member * 2 + its_core, (member, chip * 2 + its_core)
 
     def chip_peer(d):

time: 76.6 us -> 76.7 us (level)
  no operation moved by 1% of the time
where the time goes in v9:
time: 76.7 us; the launch traced here: 76.2 us
  Pallas kernels  74.2 us (97%)
  local copies, waits for them, and re-layouts  2.02 us (3%)
    pallas_call x1, Pallas kernels, on_device(): pl.pallas_call(functools.partial(kernel, groups, chips, factor), out_shap...  74.2 us
    unnamed x1, local copies, waits for them, and re-layouts  2.02 us

profile of v9, /device:TPU:0, one launch (start us, length us, event | category | flops | bytes accessed | tf_op | source)
XLA Modules:
  0.0 76.2 jit_solution(13771172099126226601)
XLA Ops:
  0.0 74.2 %shard_map.28 = f32[32,32768]{1,0:T(8,128)S(1)} custom-call(bf16[32,32768]{1,0:T(8,128)(2,1)} %x_hbm.1, f32[1,32768]{1,0:T(1,128)} %bitcast.1), custom_call_target="tpu_custom_call" | custom-call | flops 1073741824 | bytes 8388608 | tf_op jit(solution)/shard_map/pallas_call | solution.py:385
  74.2 2.0 %copy.4 = f32[32,32768]{1,0:T(8,128)} copy(f32[32,32768]{1,0:T(8,128)S(1)} %shard_map.28) | data formatting | bytes 8388608
